TPU v7x, 32 devices: a whole 2x2x4 slice. The times are simulated.
32 devices in a mesh: seq: 8 (over y, x, core), dp: 4 (over z).
Axes of the slice: x: 2, y: 2, z: 4, core: 2. Of those that a mesh axis runs over, the one named last changes fastest.
Arguments:
- frames: bfloat16 [4, 2048, 1536], P('dp', 'seq'), may hold values from -6 to 6
- lengths: int32 [4], P('dp'), may hold values from 512 to 2048, as said below
- wqkv: bfloat16 [1536, 4608], P(None, 'dp')
- wo: bfloat16 [1536, 1536], replicated, may hold values from -0.15625 to 0.15625
- gain_attn: float32 [1536], replicated, may hold values from 0.1 to 1.9
- gain_conv: float32 [1536], replicated, may hold values from 0.1 to 1.9
- conv_w: float32 [31, 1536], replicated, may hold values from -1 to 1
Outputs:
- block_out: bfloat16 [4, 2048, 1536], P('dp', 'seq')
Inputs may be any that keep to these rules, and one draw needn't show every extreme that they name: `lengths`: at least one utterance has all 2048 frames valid.
All inputs are finite; a program needn't handle non-finite values.
Results may differ from a plain program's by a relative error of at most 0.004.
The roundings to bfloat16 on the way count: a program that leaves them out, or rounds other values in their place, can miss the bound.
Values may be sent and summed in bfloat16 or wider, within the bound.
A program may use at most 64 MiB of HBM per device.

v0:
```python
import jax
import jax.numpy as jnp
from jax import lax
from jax.sharding import PartitionSpec as P

HEADS = 16


def padded_2(array, sides, width):
    for axis, dim in sides:
        count, length = (lax.axis_size(axis), array.shape[dim])
        up = [(i, (i + 1) % count) for i in range(count - 1)]
        down = [(j, i) for i, j in up]
        last = lax.slice_in_dim(array, length - width, length, axis=dim)
        leading = lax.slice_in_dim(array, 0, width, axis=dim)
        before = lax.ppermute(last, axis, up)
        after = lax.ppermute(leading, axis, down)
        array = jnp.concatenate([before, array, after], axis=dim)
    return array


def layer_norm(values, gain):
    values = values.astype(jnp.float32)
    mean = jnp.mean(values, axis=-1, keepdims=True)
    centred = values - mean
    var = jnp.mean(centred * centred, axis=-1, keepdims=True)
    return centred * lax.rsqrt(var + 1e-05) * gain


def attend(query, keys, values, length, head_size):
    scores = jnp.einsum(
        "qhe,khe->hqk", query, keys, preferred_element_type=jnp.float32
    ) * head_size ** (-0.5)
    valid = jnp.arange(keys.shape[0], dtype=jnp.int32) < length
    scores = jnp.where(valid[None, None, :], scores, -1e30)
    top = jnp.max(scores, axis=-1, keepdims=True)
    weights = jnp.exp(scores - top)
    probs = (weights / jnp.sum(weights, axis=-1, keepdims=True)).astype(jnp.bfloat16)
    return jnp.einsum("hqk,khe->qhe", probs, values, preferred_element_type=jnp.float32).astype(
        jnp.bfloat16
    )


def body(frames, lengths, wqkv, wo, gain_attn, gain_conv, conv_w):
    rows = frames[0]
    count = rows.shape[0]
    width = rows.shape[1]
    head_size = width // HEADS
    length = lengths[0]
    normed = layer_norm(rows, gain_attn).astype(jnp.bfloat16)
    qkv = jnp.dot(
        normed, lax.all_gather(wqkv, "dp", axis=1, tiled=True), preferred_element_type=jnp.float32
    ).astype(jnp.bfloat16)
    grouped = qkv.reshape(count, HEADS, 3 * head_size)
    local = lax.all_to_all(grouped, "seq", split_axis=1, concat_axis=0, tiled=True)
    total = local.shape[0]
    local_heads = local.shape[1]
    query = local[:, :, :head_size]
    keys = local[:, :, head_size : 2 * head_size]
    values = local[:, :, 2 * head_size :]
    block = 512
    query_blocks = query.reshape(total // block, block, local_heads, head_size)
    attended = lax.map(
        lambda part_rows: attend(part_rows, keys, values, length, head_size), query_blocks
    )
    attended = attended.reshape(total, local_heads, head_size)
    back = lax.all_to_all(attended, "seq", split_axis=0, concat_axis=1, tiled=True)
    heads_out = back.reshape(count, width)
    mid = rows.astype(jnp.float32) + jnp.dot(heads_out, wo, preferred_element_type=jnp.float32)
    first_frame = lax.axis_index("seq") * count
    positions = first_frame + jnp.arange(count, dtype=jnp.int32)
    valid = (positions < length).astype(jnp.float32)
    conv_in = (layer_norm(mid, gain_conv) * valid[:, None]).astype(jnp.bfloat16)
    reach = (conv_w.shape[0] - 1) // 2
    padded = padded_2(conv_in, (("seq", 0),), reach)
    conv = jnp.zeros((count, width), jnp.float32)
    for tap in range(conv_w.shape[0]):
        conv = conv + conv_w[tap][None, :] * padded[tap : tap + count].astype(jnp.float32)
    result = (mid + conv * jax.nn.sigmoid(conv)).astype(jnp.bfloat16)
    return result[None]


def solution(mesh):
    return jax.shard_map(
        body,
        mesh=mesh,
        in_specs=(P("dp", "seq", None), P("dp"), P(None, "dp"), P(), P(), P(), P()),
        out_specs=P("dp", "seq", None),
        check_vma=False,
    )
```

profile of v0, /device:TPU:3, one launch (start us, length us, event | category | flops | bytes accessed | tf_op | source)
XLA Modules:
  0.0 401.4 jit_solution(8569938863491406058)
XLA Ops:
  6.5 0.0 copy-start
  6.5 0.0 all-gather.2.cloned.1.call-start
  6.5 0.7 all-gather.2.cloned.1.call-update
  7.3 0.4 copy-done
  7.7 0.0 copy-start.4
  7.7 0.2 convert_reduce_fusion
  7.9 0.3 fusion.31
  8.2 246.1 %all-gather.2.cloned.1.call-done = bf16[1536,4608]{1,0:T(8,128)(2,1)} async-done(((bf16[1536,1152]{1,0:T(8,128)(2,1)}), bf16[1536,4608]{1,0:T(8,128)(2,1)}) %all-gather.2.cloned.1.call-update) | async-done | bytes 14155792 | tf_op jit(solution)/shard_map/all_gather | solution.py:52
  254.3 0.0 copy-done.4
  254.3 9.2 %convolution_convert_fusion = bf16[256,4608]{1,0:T(8,128)(2,1)S(1)} fusion(bf16[1536,4608]{1,0:T(8,128)(2,1)} %all-gather.2.cloned.1.call-done, bf16[1,256,1536]{2,1,0:T(8,128)(2,1)S(1)} %copy-done, f32[1536]{0:T(1024)S(1)} %copy-done.4, f32[256]{0:T(256)S(1)} %add_rsqrt_fusion.1, f32[256]{0:T(256)S(1)} %broadcast_multiply_fusion.1), kind=kOutput, calls=%fused_computation.23 | convolution fusion | flops 3627024384 | bytes 17309696 | tf_op jit(solution)/shard_map/dot_general | solution.py:51
  263.6 2.4 copy.23
  266.0 4.3 %all-to-all-start = ((bf16[256,16,288]{0,2,1:T(8,128)(2,1)}), bf16[256,16,288]{0,2,1:T(8,128)(2,1)S(1)}, u32[]{:S(2)}, u32[]{:S(2)}) async-start(bf16[256,16,288]{0,2,1:T(8,128)(2,1)} %bitcast.71), calls=%async_computation | async-start | bytes 4718592 | tf_op jit(solution)/shard_map/all_to_all | solution.py:55
  270.3 27.9 %all-to-all-done = bf16[256,16,288]{0,2,1:T(8,128)(2,1)S(1)} async-done(((bf16[256,16,288]{0,2,1:T(8,128)(2,1)}), bf16[256,16,288]{0,2,1:T(8,128)(2,1)S(1)}, u32[]{:S(2)}, u32[]{:S(2)}) %all-to-all-start) | async-done | bytes 2359328 | tf_op jit(solution)/shard_map/all_to_all | solution.py:55
  298.2 0.3 copy.35
  298.5 0.2 fusion.72
  298.7 0.0 copy-start.1
  298.8 1.0 copy.37
  299.8 0.4 copy-done.1
  300.2 50.0 %while.10 = (s32[]{:T(128)}, bf16[4,512,2,96]{1,3,2,0:T(8,128)(2,1)S(1)}, s32[]{:T(128)}, bf16[4,512,2,96]{1,3,2,0:T(8,128)(2,1)}, bf16[2048,2,96]{0,2,1:T(8,128...) while((s32[]{:T(128)}, bf16[4,512,2,96]{1,3,2,0:T(8,128)(2,1)S(1)}, s32[]{:T(128)}, ...), condition=%wide.region_5.6_spmd, body=%wide.region_2.5_spmd.sunk | while | flops 817991680 | bytes 18756180 | solution.py:63
  300.2 0.7 iota_compare_fusion.2
  300.8 6.9 %fusion.89 = (f32[2,512]{1,0:T(2,128)S(1)}, f32[2,512,2048]{2,1,0:T(8,128)}) fusion(pred[2048]{0:T(1024)(128)(4,1)S(1)} %iota_compare_fusion.2, bf16[2048,2,96]{0,2,1:T(8,128)(2,1)S(1)} %get-tuple-element.173, bf16[4,512,2,96]{1,3,2,0:T(8,128)(2,1)} %get-tuple-element.172, s32[]{:T(128)} %get-tuple-element.162), kind=kOutput, calls=%fused_computation.152.clone.1 | convolution fusion | flops 411043840 | bytes 9378304 | tf_op jit(solution)/shard_map/while/body/eval_jaxpr/sub | solution.py:37
  307.8 4.9 %fusion.90 = bf16[4,512,2,96]{1,3,2,0:T(8,128)(2,1)S(1)} fusion(bf16[4,512,2,96]{1,3,2,0:T(8,128)(2,1)S(1)} %get-tuple-element.163, s32[]{:T(128)} %get-tuple-element.162, bf16[2048,2,96]{0,2,1:T(8,128)(2,1)S(1)} %get-tuple-element.174, f32[2,512,2048]{2,1,0:T(8,128)} %get-tuple-element.153, f32[2,512]{1,0:T(2,128)S(1)} %get-tuple-element.154), kind=kOutput, calls=%fused_computation.11.clone.1 | convolution fusion | flops 406945792 | bytes 9375748 | tf_op jit(solution)/shard_map/while/body/eval_jaxpr/hqk,khe->qhe/dot_general | solution.py:39
  312.7 0.7 iota_compare_fusion.2
  313.3 6.9 %fusion.89 = (f32[2,512]{1,0:T(2,128)S(1)}, f32[2,512,2048]{2,1,0:T(8,128)}) fusion(pred[2048]{0:T(1024)(128)(4,1)S(1)} %iota_compare_fusion.2, bf16[2048,2,96]{0,2,1:T(8,128)(2,1)S(1)} %get-tuple-element.173, bf16[4,512,2,96]{1,3,2,0:T(8,128)(2,1)} %get-tuple-element.172, s32[]{:T(128)} %get-tuple-element.162), kind=kOutput, calls=%fused_computation.152.clone.1 | convolution fusion | flops 411043840 | bytes 9378304 | tf_op jit(solution)/shard_map/while/body/eval_jaxpr/sub | solution.py:37
  320.3 4.9 %fusion.90 = bf16[4,512,2,96]{1,3,2,0:T(8,128)(2,1)S(1)} fusion(bf16[4,512,2,96]{1,3,2,0:T(8,128)(2,1)S(1)} %get-tuple-element.163, s32[]{:T(128)} %get-tuple-element.162, bf16[2048,2,96]{0,2,1:T(8,128)(2,1)S(1)} %get-tuple-element.174, f32[2,512,2048]{2,1,0:T(8,128)} %get-tuple-element.153, f32[2,512]{1,0:T(2,128)S(1)} %get-tuple-element.154), kind=kOutput, calls=%fused_computation.11.clone.1 | convolution fusion | flops 406945792 | bytes 9375748 | tf_op jit(solution)/shard_map/while/body/eval_jaxpr/hqk,khe->qhe/dot_general | solution.py:39
  325.2 0.7 iota_compare_fusion.2
  325.8 6.9 %fusion.89 = (f32[2,512]{1,0:T(2,128)S(1)}, f32[2,512,2048]{2,1,0:T(8,128)}) fusion(pred[2048]{0:T(1024)(128)(4,1)S(1)} %iota_compare_fusion.2, bf16[2048,2,96]{0,2,1:T(8,128)(2,1)S(1)} %get-tuple-element.173, bf16[4,512,2,96]{1,3,2,0:T(8,128)(2,1)} %get-tuple-element.172, s32[]{:T(128)} %get-tuple-element.162), kind=kOutput, calls=%fused_computation.152.clone.1 | convolution fusion | flops 411043840 | bytes 9378304 | tf_op jit(solution)/shard_map/while/body/eval_jaxpr/sub | solution.py:37
  332.8 4.9 %fusion.90 = bf16[4,512,2,96]{1,3,2,0:T(8,128)(2,1)S(1)} fusion(bf16[4,512,2,96]{1,3,2,0:T(8,128)(2,1)S(1)} %get-tuple-element.163, s32[]{:T(128)} %get-tuple-element.162, bf16[2048,2,96]{0,2,1:T(8,128)(2,1)S(1)} %get-tuple-element.174, f32[2,512,2048]{2,1,0:T(8,128)} %get-tuple-element.153, f32[2,512]{1,0:T(2,128)S(1)} %get-tuple-element.154), kind=kOutput, calls=%fused_computation.11.clone.1 | convolution fusion | flops 406945792 | bytes 9375748 | tf_op jit(solution)/shard_map/while/body/eval_jaxpr/hqk,khe->qhe/dot_general | solution.py:39
  337.7 0.7 iota_compare_fusion.2
  338.3 6.9 %fusion.89 = (f32[2,512]{1,0:T(2,128)S(1)}, f32[2,512,2048]{2,1,0:T(8,128)}) fusion(pred[2048]{0:T(1024)(128)(4,1)S(1)} %iota_compare_fusion.2, bf16[2048,2,96]{0,2,1:T(8,128)(2,1)S(1)} %get-tuple-element.173, bf16[4,512,2,96]{1,3,2,0:T(8,128)(2,1)} %get-tuple-element.172, s32[]{:T(128)} %get-tuple-element.162), kind=kOutput, calls=%fused_computation.152.clone.1 | convolution fusion | flops 411043840 | bytes 9378304 | tf_op jit(solution)/shard_map/while/body/eval_jaxpr/sub | solution.py:37
  345.3 4.9 %fusion.90 = bf16[4,512,2,96]{1,3,2,0:T(8,128)(2,1)S(1)} fusion(bf16[4,512,2,96]{1,3,2,0:T(8,128)(2,1)S(1)} %get-tuple-element.163, s32[]{:T(128)} %get-tuple-element.162, bf16[2048,2,96]{0,2,1:T(8,128)(2,1)S(1)} %get-tuple-element.174, f32[2,512,2048]{2,1,0:T(8,128)} %get-tuple-element.153, f32[2,512]{1,0:T(2,128)S(1)} %get-tuple-element.154), kind=kOutput, calls=%fused_computation.11.clone.1 | convolution fusion | flops 406945792 | bytes 9375748 | tf_op jit(solution)/shard_map/while/body/eval_jaxpr/hqk,khe->qhe/dot_general | solution.py:39
  350.2 0.0 copy-start.2
  350.2 2.0 copy.30
  352.2 5.1 %all-to-all-start.1 = ((bf16[2048,2,96]{2,1,0:T(2,128)(2,1)}), bf16[2048,2,96]{2,1,0:T(2,128)(2,1)S(1)}, u32[]{:S(2)}, u32[]{:S(2)}) async-start(bf16[2048,2,96]{2,1,0:T(2,128)(2,1)} %bitcast.8), calls=%async_computation.1 | async-start | bytes 2097152 | tf_op jit(solution)/shard_map/all_to_all | solution.py:67
  357.9 0.0 copy-done.2
  357.9 0.3 slice_reduce_fusion.30
  358.2 12.8 %all-to-all-done.1 = bf16[2048,2,96]{2,1,0:T(2,128)(2,1)S(1)} async-done(((bf16[2048,2,96]{2,1,0:T(2,128)(2,1)}), bf16[2048,2,96]{2,1,0:T(2,128)(2,1)S(1)}, u32[]{:S(2)}, u32[]{:S(2)}) %all-to-all-start.1) | async-done | bytes 786464 | tf_op jit(solution)/shard_map/all_to_all | solution.py:67
  371.1 0.7 copy.32
  371.7 3.8 fusion.74
  375.6 0.0 copy-start.3
  375.6 0.3 multiply_reduce_fusion
  375.9 0.4 copy-done.3
  376.3 0.4 multiply_convert_fusion
  376.7 3.5 collective-permute-start
  380.1 1.9 collective-permute-start.1
  382.1 0.2 slice_reduce_fusion.29
  382.3 0.0 collective-permute-done
  382.3 4.2 %collective-permute-done.1 = bf16[15,1536]{1,0:T(8,128)(2,1)S(1)} collective-permute-done((bf16[15,1536]{1,0:T(8,128)(2,1)S(1)}, bf16[15,1536]{1,0:T(8,128)(2,1)S(1)}, u32[]{:S(2)}, u32[]{:S(2)}) %collective-permute-start.1) | collective-permute-done | bytes 46112 | tf_op jit(solution)/shard_map/ppermute | solution.py:17
  386.4 8.2 %fusion.66 = bf16[1,256,1536]{2,1,0:T(8,128)(2,1)} fusion(f32[256,1536]{1,0:T(8,128)S(1)} %get-tuple-element.113, bf16[15,1536]{1,0:T(8,128)(2,1)S(1)} %collective-permute-done.1, bf16[256,1536]{1,0:T(8,128)(2,1)S(1)} %multiply_convert_fusion, f32[1536]{0:T(1024)S(1)} %get-tuple-element.91, f32[1536]{0:T(1024)S(1)} %get-tuple-element.92, ...), kind=kLoop, calls=%fused_computation.115 | loop fusion | flops 73924608 | bytes 3428352 | tf_op jit(solution)/shard_map/broadcast_in_dim | solution.py:80
  (7 shorter events, 0.0 us)
Async XLA Ops:
  6.5 1.1 copy-start
  6.5 247.8 %all-gather.2.cloned.1.call-start = ((), (), s32[]{:S(2)}) async-start(), calls=%async_computation.2 | async-start | bytes 17694720 | tf_op jit(solution)/shard_map/all_gather | solution.py:52
  7.7 246.7 %copy-start.4 = (f32[1536]{0:T(1024)S(1)}, f32[1536]{0:T(1024)}, u32[]{:S(2)}) copy-start(f32[1536]{0:T(1024)} %param.13) | copy-start | bytes 18436
  266.0 32.2 %all-to-all-start = ((bf16[256,16,288]{0,2,1:T(8,128)(2,1)}), bf16[256,16,288]{0,2,1:T(8,128)(2,1)S(1)}, u32[]{:S(2)}, u32[]{:S(2)}) async-start(bf16[256,16,288]{0,2,1:T(8,128)(2,1)} %bitcast.71), calls=%async_computation | async-start | bytes 4718592 | tf_op jit(solution)/shard_map/all_to_all | solution.py:55
  298.7 1.4 copy-start.1
  350.2 7.7 %copy-start.2 = (f32[31,1536]{1,0:T(8,128)S(1)}, f32[31,1536]{1,0:T(8,128)}, u32[]{:S(2)}) copy-start(f32[31,1536]{1,0:T(8,128)} %param.15) | copy-start | bytes 571396
  352.2 18.9 %all-to-all-start.1 = ((bf16[2048,2,96]{2,1,0:T(2,128)(2,1)}), bf16[2048,2,96]{2,1,0:T(2,128)(2,1)S(1)}, u32[]{:S(2)}, u32[]{:S(2)}) async-start(bf16[2048,2,96]{2,1,0:T(2,128)(2,1)} %bitcast.8), calls=%async_computation.1 | async-start | bytes 2097152 | tf_op jit(solution)/shard_map/all_to_all | solution.py:67
  375.6 0.7 copy-start.3
  376.7 5.6 %collective-permute-start = (bf16[15,1536]{1,0:T(8,128)(2,1)S(1)}, bf16[15,1536]{1,0:T(8,128)(2,1)S(1)}, u32[]{:S(2)}, u32[]{:S(2)}) collective-permute-start(bf16[15,1536]{1,0:T(8,128)(2,1)S(1)} %get-tuple-element.110), channel_id=1, source_target_pairs={{0,4},{4,8},{8,12},{12,16},{16,20},{20,24},{24,28},{1,5},{5,9},{9,... | collective-permute-start | bytes 138248 | tf_op jit(solution)/shard_map/ppermute | solution.py:16
  380.1 6.3 %collective-permute-start.1 = (bf16[15,1536]{1,0:T(8,128)(2,1)S(1)}, bf16[15,1536]{1,0:T(8,128)(2,1)S(1)}, u32[]{:S(2)}, u32[]{:S(2)}) collective-permute-start(bf16[15,1536]{1,0:T(8,128)(2,1)S(1)} %get-tuple-element.111), channel_id=1, source_target_pairs={{4,0},{8,4},{12,8},{16,12},{20,16},{24,20},{28,24},{5,1},{9,5},{13... | collective-permute-start | bytes 138248 | tf_op jit(solution)/shard_map/ppermute | solution.py:17
Sparse Core Ops, SparseCore 0:
  8.9 245.3 all-gather.1
where the time goes:
time: 402 us; the launch traced here: 401 us
  waiting for transfers between devices  292 us (73%)
  matrix products  60.3 us (15%)
  starting transfers between devices  14.7 us (4%)
  between operations  14.2 us (4%)
  other arithmetic  12 us (3%)
  local copies, waits for them, and re-layouts  8.37 us (2%)
    all_gather x1, waiting for transfers between devices, body(): lax.all_gather(wqkv, 'dp', axis=1, tiled=True)  246 us
    all_to_all x1, waiting for transfers between devices, body(): lax.all_to_all(grouped, 'seq', split_axis=1, concat_axis=0, tiled=True)  27.9 us
    sub x4, matrix products, attend(): weights = jnp.exp(scores - top)  27.7 us
    dot_general x4, matrix products, attend(): jnp.einsum('hqk,khe->qhe', probs, values, preferred_element_type=jnp.floa...  19.6 us
    all_to_all x1, waiting for transfers between devices, body(): lax.all_to_all(attended, 'seq', split_axis=0, concat_axis=1, tiled=True)  12.8 us
    dot_general x1, matrix products, body(): jnp.dot(normed, lax.all_gather(wqkv, 'dp', axis=1, tiled=True), preferred...  9.23 us
    broadcast_in_dim x1, other arithmetic, body(): return result[None]  8.17 us
  transfers between devices with their start and end apart: 5, of which 4 were waited for; matrix products, arithmetic and copies ran while one was open for 0% of the time, Pallas kernels for 0%

commit v1 on v0

--- a/solution.py
+++ b/solution.py
@@ -4,6 +4,30 @@
 from jax.sharding import PartitionSpec as P
 
 HEADS = 16
+
+
+def plan_trees_by_axis(local_values):
+    f_next = lax.axis_size("seq")
+    arr_next, y = (f_next, lax.axis_index("seq"))
+    known = local_values.shape[0] // arr_next
+    small = list(local_values.shape)
+    small[0] = known
+    u1 = small[1]
+    small[1] = u1 * arr_next
+    carry_in = jnp.zeros(small, local_values.dtype)
+    rr = 0
+    while rr < arr_next:
+        w1 = lax.dynamic_slice_in_dim(local_values, (y ^ rr) * known, known, axis=0)
+        if rr:
+            cards = []
+            dev = 0
+            while dev < arr_next:
+                cards.append((dev, dev ^ rr))
+                dev = dev + 1
+            w1 = lax.ppermute(w1, axis_name="seq", perm=cards)
+        carry_in = lax.dynamic_update_slice_in_dim(carry_in, w1, (y ^ rr) * u1, axis=1)
+        rr += 1
+    return carry_in
 
 
 def padded_2(array, sides, width):
@@ -64,7 +88,7 @@
         lambda part_rows: attend(part_rows, keys, values, length, head_size), query_blocks
     )
     attended = attended.reshape(total, local_heads, head_size)
-    back = lax.all_to_all(attended, "seq", split_axis=0, concat_axis=1, tiled=True)
+    back = plan_trees_by_axis(attended)
     heads_out = back.reshape(count, width)
     mid = rows.astype(jnp.float32) + jnp.dot(heads_out, wo, preferred_element_type=jnp.float32)
     first_frame = lax.axis_index("seq") * count

time: 402 us -> 394 us (0.980)
  waiting for transfers between devices: 292 us -> 284 us
    all_to_all x1 -> x0, waiting for transfers between devices: 12.8 us -> none  [body(): lax.all_to_all(attended, 'seq', split_axis=0, concat_axis=1, tiled=True)]
    ppermute x0 -> x7, starting transfers between devices: none -> 7.28 us  [plan_trees_by_axis(): w1 = lax.ppermute(w1, axis_name='seq', perm=cards)]
    ppermute x0 -> x7, waiting for transfers between devices: none -> 5.72 us  [plan_trees_by_axis(): w1 = lax.ppermute(w1, axis_name='seq', perm=cards)]
    all_to_all x1 -> x0, starting transfers between devices: 5.06 us -> none  [body(): lax.all_to_all(attended, 'seq', split_axis=0, concat_axis=1, tiled=True)]
  transfers between devices with their start and end apart: 5 -> 11, of which waited for: 4 -> 5; matrix products, arithmetic and copies ran while one was open for 0% -> 0% of each run, Pallas kernels for 0% -> 0%
where the time goes in v1:
time: 394 us; the launch traced here: 393 us
  waiting for transfers between devices  284 us (72%)
  matrix products  60.6 us (15%)
  starting transfers between devices  16.8 us (4%)
  between operations  14.3 us (4%)
  other arithmetic  12 us (3%)
  local copies, waits for them, and re-layouts  6.06 us (2%)
    all_gather x1, waiting for transfers between devices, body(): lax.all_gather(wqkv, 'dp', axis=1, tiled=True)  246 us
    sub x4, matrix products, attend(): weights = jnp.exp(scores - top)  27.8 us
    all_to_all x1, waiting for transfers between devices, body(): lax.all_to_all(grouped, 'seq', split_axis=1, concat_axis=0, tiled=True)  26.8 us
    dot_general x4, matrix products, attend(): jnp.einsum('hqk,khe->qhe', probs, values, preferred_element_type=jnp.floa...  19.7 us
    dot_general x1, matrix products, body(): jnp.dot(normed, lax.all_gather(wqkv, 'dp', axis=1, tiled=True), preferred...  9.24 us
    broadcast_in_dim x1, other arithmetic, body(): return result[None]  8.17 us
  transfers between devices with their start and end apart: 11, of which 5 were waited for; matrix products, arithmetic and copies ran while one was open for 0% of the time, Pallas kernels for 0%

profile of v1, /device:TPU:3, one launch (start us, length us, event | category | flops | bytes accessed | tf_op | source)
XLA Modules:
  0.0 393.4 jit_solution(12702874478678972580)
XLA Ops:
  6.5 0.0 copy-start
  6.5 0.0 all-gather.2.cloned.1.call-start
  6.5 0.7 all-gather.2.cloned.1.call-update
  7.3 0.4 copy-done
  7.7 0.0 copy-start.4
  7.7 0.2 convert_reduce_fusion
  7.9 0.3 fusion.31
  8.2 246.1 %all-gather.2.cloned.1.call-done = bf16[1536,4608]{1,0:T(8,128)(2,1)} async-done(((bf16[1536,1152]{1,0:T(8,128)(2,1)}), bf16[1536,4608]{1,0:T(8,128)(2,1)}) %all-gather.2.cloned.1.call-update) | async-done | bytes 14155792 | tf_op jit(solution)/shard_map/all_gather | solution.py:76
  254.3 0.0 copy-done.4
  254.3 9.2 %convolution_convert_fusion = bf16[256,4608]{1,0:T(8,128)(2,1)S(1)} fusion(bf16[1536,4608]{1,0:T(8,128)(2,1)} %all-gather.2.cloned.1.call-done, bf16[1,256,1536]{2,1,0:T(8,128)(2,1)S(1)} %copy-done, f32[1536]{0:T(1024)S(1)} %copy-done.4, f32[256]{0:T(256)S(1)} %add_rsqrt_fusion.1, f32[256]{0:T(256)S(1)} %broadcast_multiply_fusion.1), kind=kOutput, calls=%fused_computation.23 | convolution fusion | flops 3627024384 | bytes 17309696 | tf_op jit(solution)/shard_map/dot_general | solution.py:75
  263.6 2.4 copy.12
  266.0 0.0 copy-start.2
  266.0 4.4 %all-to-all-start = ((bf16[256,16,288]{0,2,1:T(8,128)(2,1)}), bf16[256,16,288]{0,2,1:T(8,128)(2,1)S(1)}, u32[]{:S(2)}, u32[]{:S(2)}) async-start(bf16[256,16,288]{0,2,1:T(8,128)(2,1)} %bitcast.68), calls=%async_computation | async-start | bytes 4718592 | tf_op jit(solution)/shard_map/all_to_all | solution.py:79
  271.2 0.0 copy-done.2
  271.2 0.3 slice_reduce_fusion.30
  271.5 26.8 %all-to-all-done = bf16[256,16,288]{0,2,1:T(8,128)(2,1)S(1)} async-done(((bf16[256,16,288]{0,2,1:T(8,128)(2,1)}), bf16[256,16,288]{0,2,1:T(8,128)(2,1)S(1)}, u32[]{:S(2)}, u32[]{:S(2)}) %all-to-all-start) | async-done | bytes 2359328 | tf_op jit(solution)/shard_map/all_to_all | solution.py:79
  298.3 0.3 copy.17
  298.6 0.2 fusion.72
  298.9 0.0 copy-start.1
  298.9 1.0 copy.20
  299.9 0.4 copy-done.1
  300.3 50.2 %while.10 = (s32[]{:T(128)}, bf16[4,512,2,96]{1,3,2,0:T(8,128)(2,1)S(1)}, s32[]{:T(128)}, bf16[4,512,2,96]{1,3,2,0:T(8,128)(2,1)}, bf16[2048,2,96]{0,2,1:T(8,128...) while((s32[]{:T(128)}, bf16[4,512,2,96]{1,3,2,0:T(8,128)(2,1)S(1)}, s32[]{:T(128)}, ...), condition=%wide.region_5.6_spmd, body=%wide.region_2.5_spmd.sunk | while | flops 817991680 | bytes 18756180 | solution.py:87
  300.3 0.7 iota_compare_fusion.2
  300.9 7.0 %fusion.89 = (f32[2,512]{1,0:T(2,128)S(1)}, f32[2,512,2048]{2,1,0:T(8,128)}) fusion(pred[2048]{0:T(1024)(128)(4,1)S(1)} %iota_compare_fusion.2, bf16[2048,2,96]{0,2,1:T(8,128)(2,1)S(1)} %get-tuple-element.169, bf16[4,512,2,96]{1,3,2,0:T(8,128)(2,1)} %get-tuple-element.168, s32[]{:T(128)} %get-tuple-element.158), kind=kOutput, calls=%fused_computation.167.clone.1 | convolution fusion | flops 411043840 | bytes 9378304 | tf_op jit(solution)/shard_map/while/body/eval_jaxpr/sub | solution.py:61
  307.9 4.9 %fusion.90 = bf16[4,512,2,96]{1,3,2,0:T(8,128)(2,1)S(1)} fusion(bf16[4,512,2,96]{1,3,2,0:T(8,128)(2,1)S(1)} %get-tuple-element.159, s32[]{:T(128)} %get-tuple-element.158, bf16[2048,2,96]{0,2,1:T(8,128)(2,1)S(1)} %get-tuple-element.170, f32[2,512,2048]{2,1,0:T(8,128)} %get-tuple-element.149, f32[2,512]{1,0:T(2,128)S(1)} %get-tuple-element.150), kind=kOutput, calls=%fused_computation.11.clone.1 | convolution fusion | flops 406945792 | bytes 9375748 | tf_op jit(solution)/shard_map/while/body/eval_jaxpr/hqk,khe->qhe/dot_general | solution.py:63
  312.8 0.7 iota_compare_fusion.2
  313.5 7.0 %fusion.89 = (f32[2,512]{1,0:T(2,128)S(1)}, f32[2,512,2048]{2,1,0:T(8,128)}) fusion(pred[2048]{0:T(1024)(128)(4,1)S(1)} %iota_compare_fusion.2, bf16[2048,2,96]{0,2,1:T(8,128)(2,1)S(1)} %get-tuple-element.169, bf16[4,512,2,96]{1,3,2,0:T(8,128)(2,1)} %get-tuple-element.168, s32[]{:T(128)} %get-tuple-element.158), kind=kOutput, calls=%fused_computation.167.clone.1 | convolution fusion | flops 411043840 | bytes 9378304 | tf_op jit(solution)/shard_map/while/body/eval_jaxpr/sub | solution.py:61
  320.5 4.9 %fusion.90 = bf16[4,512,2,96]{1,3,2,0:T(8,128)(2,1)S(1)} fusion(bf16[4,512,2,96]{1,3,2,0:T(8,128)(2,1)S(1)} %get-tuple-element.159, s32[]{:T(128)} %get-tuple-element.158, bf16[2048,2,96]{0,2,1:T(8,128)(2,1)S(1)} %get-tuple-element.170, f32[2,512,2048]{2,1,0:T(8,128)} %get-tuple-element.149, f32[2,512]{1,0:T(2,128)S(1)} %get-tuple-element.150), kind=kOutput, calls=%fused_computation.11.clone.1 | convolution fusion | flops 406945792 | bytes 9375748 | tf_op jit(solution)/shard_map/while/body/eval_jaxpr/hqk,khe->qhe/dot_general | solution.py:63
  325.4 0.7 iota_compare_fusion.2
  326.0 7.0 %fusion.89 = (f32[2,512]{1,0:T(2,128)S(1)}, f32[2,512,2048]{2,1,0:T(8,128)}) fusion(pred[2048]{0:T(1024)(128)(4,1)S(1)} %iota_compare_fusion.2, bf16[2048,2,96]{0,2,1:T(8,128)(2,1)S(1)} %get-tuple-element.169, bf16[4,512,2,96]{1,3,2,0:T(8,128)(2,1)} %get-tuple-element.168, s32[]{:T(128)} %get-tuple-element.158), kind=kOutput, calls=%fused_computation.167.clone.1 | convolution fusion | flops 411043840 | bytes 9378304 | tf_op jit(solution)/shard_map/while/body/eval_jaxpr/sub | solution.py:61
  333.0 4.9 %fusion.90 = bf16[4,512,2,96]{1,3,2,0:T(8,128)(2,1)S(1)} fusion(bf16[4,512,2,96]{1,3,2,0:T(8,128)(2,1)S(1)} %get-tuple-element.159, s32[]{:T(128)} %get-tuple-element.158, bf16[2048,2,96]{0,2,1:T(8,128)(2,1)S(1)} %get-tuple-element.170, f32[2,512,2048]{2,1,0:T(8,128)} %get-tuple-element.149, f32[2,512]{1,0:T(2,128)S(1)} %get-tuple-element.150), kind=kOutput, calls=%fused_computation.11.clone.1 | convolution fusion | flops 406945792 | bytes 9375748 | tf_op jit(solution)/shard_map/while/body/eval_jaxpr/hqk,khe->qhe/dot_general | solution.py:63
  337.9 0.7 iota_compare_fusion.2
  338.6 7.0 %fusion.89 = (f32[2,512]{1,0:T(2,128)S(1)}, f32[2,512,2048]{2,1,0:T(8,128)}) fusion(pred[2048]{0:T(1024)(128)(4,1)S(1)} %iota_compare_fusion.2, bf16[2048,2,96]{0,2,1:T(8,128)(2,1)S(1)} %get-tuple-element.169, bf16[4,512,2,96]{1,3,2,0:T(8,128)(2,1)} %get-tuple-element.168, s32[]{:T(128)} %get-tuple-element.158), kind=kOutput, calls=%fused_computation.167.clone.1 | convolution fusion | flops 411043840 | bytes 9378304 | tf_op jit(solution)/shard_map/while/body/eval_jaxpr/sub | solution.py:61
  345.6 4.9 %fusion.90 = bf16[4,512,2,96]{1,3,2,0:T(8,128)(2,1)S(1)} fusion(bf16[4,512,2,96]{1,3,2,0:T(8,128)(2,1)S(1)} %get-tuple-element.159, s32[]{:T(128)} %get-tuple-element.158, bf16[2048,2,96]{0,2,1:T(8,128)(2,1)S(1)} %get-tuple-element.170, f32[2,512,2048]{2,1,0:T(8,128)} %get-tuple-element.149, f32[2,512]{1,0:T(2,128)S(1)} %get-tuple-element.150), kind=kOutput, calls=%fused_computation.11.clone.1 | convolution fusion | flops 406945792 | bytes 9375748 | tf_op jit(solution)/shard_map/while/body/eval_jaxpr/hqk,khe->qhe/dot_general | solution.py:63
  350.5 0.1 copy.18
  350.6 0.1 broadcast_in_dim.25
  350.7 0.1 constant_dynamic-slice_fusion
  350.8 0.5 collective-permute-start
  351.3 1.2 collective-permute-start.1
  352.6 0.5 collective-permute-start.2
  353.0 0.4 collective-permute-start.3
  353.4 1.4 collective-permute-start.4
  354.8 0.0 collective-permute-done
  354.8 1.2 collective-permute-start.5
  356.1 0.0 collective-permute-done.1
  356.1 2.0 collective-permute-start.6
  358.1 0.6 collective-permute-done.2
  358.7 0.0 collective-permute-done.3
  358.8 5.1 %collective-permute-done.4 = bf16[256,2,96]{0,2,1:T(8,128)(2,1)S(1)} collective-permute-done((bf16[256,2,96]{0,2,1:T(8,128)(2,1)S(1)}, bf16[256,2,96]{0,2,1:T(8,128)(2,1)S(1)}, u32[]{:S(2)}, u32[]{:S(2)}) %collective-permute-start.4) | collective-permute-done | bytes 98336 | tf_op jit(solution)/shard_map/ppermute | solution.py:27
  363.9 0.0 collective-permute-done.5
  363.9 0.0 collective-permute-done.6
  364.0 3.8 fusion.74
  367.8 0.0 copy-start.3
  367.8 0.3 multiply_reduce_fusion
  368.1 0.4 copy-done.3
  368.5 0.4 multiply_convert_fusion
  368.9 3.1 collective-permute-start.7
  372.0 1.9 collective-permute-start.8
  374.0 0.2 slice_reduce_fusion.29
  374.2 0.0 collective-permute-done.7
  374.2 4.2 %collective-permute-done.8 = bf16[15,1536]{1,0:T(8,128)(2,1)S(1)} collective-permute-done((bf16[15,1536]{1,0:T(8,128)(2,1)S(1)}, bf16[15,1536]{1,0:T(8,128)(2,1)S(1)}, u32[]{:S(2)}, u32[]{:S(2)}) %collective-permute-start.8) | collective-permute-done | bytes 46112 | tf_op jit(solution)/shard_map/ppermute | solution.py:41
  378.3 8.2 %fusion.66 = bf16[1,256,1536]{2,1,0:T(8,128)(2,1)} fusion(f32[256,1536]{1,0:T(8,128)S(1)} %get-tuple-element.109, bf16[15,1536]{1,0:T(8,128)(2,1)S(1)} %collective-permute-done.8, bf16[256,1536]{1,0:T(8,128)(2,1)S(1)} %multiply_convert_fusion, f32[1536]{0:T(1024)S(1)} %get-tuple-element.79, f32[1536]{0:T(1024)S(1)} %get-tuple-element.80, ...), kind=kLoop, calls=%fused_computation.115 | loop fusion | flops 73924608 | bytes 3428352 | tf_op jit(solution)/shard_map/broadcast_in_dim | solution.py:104
  (14 shorter events, 0.1 us)
Async XLA Ops:
  6.5 1.1 copy-start
  6.5 247.8 %all-gather.2.cloned.1.call-start = ((), (), s32[]{:S(2)}) async-start(), calls=%async_computation.1 | async-start | bytes 17694720 | tf_op jit(solution)/shard_map/all_gather | solution.py:76
  7.7 246.7 %copy-start.4 = (f32[1536]{0:T(1024)S(1)}, f32[1536]{0:T(1024)}, u32[]{:S(2)}) copy-start(f32[1536]{0:T(1024)} %param.13) | copy-start | bytes 18436
  266.0 5.2 %copy-start.2 = (f32[31,1536]{1,0:T(8,128)S(1)}, f32[31,1536]{1,0:T(8,128)}, u32[]{:S(2)}) copy-start(f32[31,1536]{1,0:T(8,128)} %param.15) | copy-start | bytes 571396
  266.0 32.3 %all-to-all-start = ((bf16[256,16,288]{0,2,1:T(8,128)(2,1)}), bf16[256,16,288]{0,2,1:T(8,128)(2,1)S(1)}, u32[]{:S(2)}, u32[]{:S(2)}) async-start(bf16[256,16,288]{0,2,1:T(8,128)(2,1)} %bitcast.68), calls=%async_computation | async-start | bytes 4718592 | tf_op jit(solution)/shard_map/all_to_all | solution.py:79
  298.9 1.4 copy-start.1
  350.8 4.0 %collective-permute-start = (bf16[256,2,96]{0,2,1:T(8,128)(2,1)S(1)}, bf16[256,2,96]{0,2,1:T(8,128)(2,1)S(1)}, u32[]{:S(2)}, u32[]{:S(2)}) collective-permute-start(bf16[256,2,96]{0,2,1:T(8,128)(2,1)S(1)} %get-tuple-element.106), channel_id=1, source_target_pairs={{0,4},{4,0},{8,12},{12,8},{16,20},{20,16},{24,28},{28,24},{1,5},{5... | collective-permute-start | bytes 294920 | tf_op jit(solution)/shard_map/ppermute | solution.py:27
  351.3 4.7 %collective-permute-start.1 = (bf16[256,2,96]{0,2,1:T(8,128)(2,1)S(1)}, bf16[256,2,96]{0,2,1:T(8,128)(2,1)S(1)}, u32[]{:S(2)}, u32[]{:S(2)}) collective-permute-start(bf16[256,2,96]{0,2,1:T(8,128)(2,1)S(1)} %get-tuple-element.105), channel_id=1, source_target_pairs={{0,8},{4,12},{8,0},{12,4},{16,24},{20,28},{24,16},{28,20},{1,9},{5... | collective-permute-start | bytes 294920 | tf_op jit(solution)/shard_map/ppermute | solution.py:27
  352.6 6.2 %collective-permute-start.2 = (bf16[256,2,96]{0,2,1:T(8,128)(2,1)S(1)}, bf16[256,2,96]{0,2,1:T(8,128)(2,1)S(1)}, u32[]{:S(2)}, u32[]{:S(2)}) collective-permute-start(bf16[256,2,96]{0,2,1:T(8,128)(2,1)S(1)} %get-tuple-element.104), channel_id=1, source_target_pairs={{0,12},{4,8},{8,4},{12,0},{16,28},{20,24},{24,20},{28,16},{1,13},{... | collective-permute-start | bytes 294920 | tf_op jit(solution)/shard_map/ppermute | solution.py:27
  353.0 5.7 %collective-permute-start.3 = (bf16[256,2,96]{0,2,1:T(8,128)(2,1)S(1)}, bf16[256,2,96]{0,2,1:T(8,128)(2,1)S(1)}, u32[]{:S(2)}, u32[]{:S(2)}) collective-permute-start(bf16[256,2,96]{0,2,1:T(8,128)(2,1)S(1)} %get-tuple-element.103), channel_id=1, source_target_pairs={{0,16},{4,20},{8,24},{12,28},{16,0},{20,4},{24,8},{28,12},{1,17},{... | collective-permute-start | bytes 294920 | tf_op jit(solution)/shard_map/ppermute | solution.py:27
  353.4 10.5 %collective-permute-start.4 = (bf16[256,2,96]{0,2,1:T(8,128)(2,1)S(1)}, bf16[256,2,96]{0,2,1:T(8,128)(2,1)S(1)}, u32[]{:S(2)}, u32[]{:S(2)}) collective-permute-start(bf16[256,2,96]{0,2,1:T(8,128)(2,1)S(1)} %get-tuple-element.102), channel_id=1, source_target_pairs={{0,20},{4,16},{8,28},{12,24},{16,4},{20,0},{24,12},{28,8},{1,21},{... | collective-permute-start | bytes 294920 | tf_op jit(solution)/shard_map/ppermute | solution.py:27
  354.8 9.1 %collective-permute-start.5 = (bf16[256,2,96]{0,2,1:T(8,128)(2,1)S(1)}, bf16[256,2,96]{0,2,1:T(8,128)(2,1)S(1)}, u32[]{:S(2)}, u32[]{:S(2)}) collective-permute-start(bf16[256,2,96]{0,2,1:T(8,128)(2,1)S(1)} %get-tuple-element.101), channel_id=1, source_target_pairs={{0,24},{4,28},{8,16},{12,20},{16,8},{20,12},{24,0},{28,4},{1,25},{... | collective-permute-start | bytes 294920 | tf_op jit(solution)/shard_map/ppermute | solution.py:27
  356.1 7.9 %collective-permute-start.6 = (bf16[256,2,96]{0,2,1:T(8,128)(2,1)S(1)}, bf16[256,2,96]{0,2,1:T(8,128)(2,1)S(1)}, u32[]{:S(2)}, u32[]{:S(2)}) collective-permute-start(bf16[256,2,96]{0,2,1:T(8,128)(2,1)S(1)} %get-tuple-element.100), channel_id=1, source_target_pairs={{0,28},{4,24},{8,20},{12,16},{16,12},{20,8},{24,4},{28,0},{1,29},{... | collective-permute-start | bytes 294920 | tf_op jit(solution)/shard_map/ppermute | solution.py:27
  367.8 0.7 copy-start.3
  368.9 5.3 %collective-permute-start.7 = (bf16[15,1536]{1,0:T(8,128)(2,1)S(1)}, bf16[15,1536]{1,0:T(8,128)(2,1)S(1)}, u32[]{:S(2)}, u32[]{:S(2)}) collective-permute-start(bf16[15,1536]{1,0:T(8,128)(2,1)S(1)} %get-tuple-element.98), channel_id=1, source_target_pairs={{0,4},{4,8},{8,12},{12,16},{16,20},{20,24},{24,28},{1,5},{5,9},{9,... | collective-permute-start | bytes 138248 | tf_op jit(solution)/shard_map/ppermute | solution.py:40
  372.0 6.3 %collective-permute-start.8 = (bf16[15,1536]{1,0:T(8,128)(2,1)S(1)}, bf16[15,1536]{1,0:T(8,128)(2,1)S(1)}, u32[]{:S(2)}, u32[]{:S(2)}) collective-permute-start(bf16[15,1536]{1,0:T(8,128)(2,1)S(1)} %get-tuple-element.99), channel_id=1, source_target_pairs={{4,0},{8,4},{12,8},{16,12},{20,16},{24,20},{28,24},{5,1},{9,5},{13... | collective-permute-start | bytes 138248 | tf_op jit(solution)/shard_map/ppermute | solution.py:41
Sparse Core Ops, SparseCore 0:
  8.9 245.3 all-gather.1
